TPU v7x, 32 devices: a whole 2x2x4 slice. The times are simulated.
32 devices in a mesh: owner: 8 (over z, y), blk: 4 (over x, core).
Axes of the slice: x: 2, y: 2, z: 4, core: 2. Of those that a mesh axis runs over, the one named last changes fastest.
Arguments:
- entity_table: bfloat16 [32768, 256], P('owner'), may hold values from -1.5 to 1.5
- relations: bfloat16 [8, 256, 256], replicated, may hold values from -0.375 to 0.375
- head_ids: int32 [32768], P(('owner', 'blk')), may hold values from 0 to 32767, as said below
- rel_ids: int32 [32768], P(('owner', 'blk')), may hold values from 0 to 7
- tail_ids: int32 [32768], P(('owner', 'blk')), may hold values from 0 to 32767, as said below
- neg_ids: int32 [16384], P(('owner', 'blk')), may hold values from 0 to 32767, as said below
Outputs:
- entity_grad: float32 [32768, 256], P(('owner', 'blk'))
- relation_grad: float32 [8, 256, 256], P('blk')
Inputs may be any that keep to these rules, and one draw needn't show every extreme that they name: An entity is held by the owner index whose shard of entity_table contains its row. A device's ids are its own shards of head_ids, tail_ids and neg_ids together. Of these ids every owner holds at most 800 (800), and some owner holds exactly 800; that owner is the same for all devices of one blk index. `tail_ids`: as for head_ids: the same bound of 800 ids of one device for one owner, over the device's heads, tails and negatives together. `neg_ids`: as for head_ids: the same bound of 800 ids of one device for one owner, over the device's heads, tails and negatives together.
All inputs are finite; a program needn't handle non-finite values.
Results may differ from a plain program's by a relative error of at most 0.0027.
Values may be sent and summed in bfloat16 or wider, within the bound.
A program may use at most 64 MiB of HBM per device.

v0:
```python
import jax
import jax.numpy as jnp
from jax import lax
from jax.sharding import PartitionSpec as P


def passed_along(block, axis, distance):
    devices = range(lax.axis_size(axis))
    route = [((i - distance) % len(devices), i) for i in devices]
    return lax.ppermute(block, axis, route)


def shards(entity_table, relations, head_ids, rel_ids, tail_ids, neg_ids):
    owner_count = lax.axis_size("owner")
    cycle_count = lax.axis_size("blk")
    entity_rows, feature_count = entity_table.shape
    triple_count = head_ids.shape[0]
    negative_count = neg_ids.shape[0]
    relation_count = relations.shape[0]
    wanted = jnp.concatenate([head_ids, tail_ids, neg_ids])
    wanted_count = wanted.shape[0]
    capacity = 5 * wanted_count // (2 * owner_count)
    owners = wanted // entity_rows
    local_rows = wanted % entity_rows
    onehot = (owners[:, None] == jnp.arange(owner_count, dtype=jnp.int32)[None, :]).astype(
        jnp.int32
    )
    before = jnp.cumsum(onehot, axis=0) - onehot
    slot_index = jnp.sum(before * onehot, axis=1)
    target = owners * capacity + slot_index
    requests = jnp.zeros((owner_count * capacity,), jnp.int32).at[target].set(local_rows)
    requests = requests.reshape(owner_count, capacity)
    asked_rows = lax.all_to_all(requests, "owner", split_axis=0, concat_axis=0, tiled=True)
    found_rows = jnp.take(entity_table, asked_rows, axis=0)
    fetched, asked_rows = (
        lax.all_to_all(found_rows, "owner", split_axis=0, concat_axis=0, tiled=True),
        asked_rows,
    )
    fetched_rows = fetched.reshape(owner_count * capacity, feature_count)[target]
    head_rows = fetched_rows[:triple_count]
    tail_rows = fetched_rows[triple_count : 2 * triple_count]
    negative_rows = fetched_rows[2 * triple_count :]
    relation_hot = (
        rel_ids[:, None] == jnp.arange(relation_count, dtype=jnp.int32)[None, :]
    ).astype(jnp.bfloat16)
    spread_heads = (head_rows[:, None, :] * relation_hot[:, :, None]).reshape(
        triple_count, relation_count * feature_count
    )
    flat_relations = relations.reshape(relation_count * feature_count, feature_count)
    queries = jnp.dot(spread_heads, flat_relations, preferred_element_type=jnp.float32).astype(
        jnp.bfloat16
    )
    positive = jnp.einsum("id,id->i", queries, tail_rows, preferred_element_type=jnp.float32)
    slopes = -jax.nn.sigmoid(-positive)
    scale_neg = (cycle_count * negative_count) ** (-0.5)
    partner = slopes[:, None] * tail_rows.astype(jnp.float32)
    contract_rows = (((0,), (0,)), ((), ()))
    contract_cols = (((1,), (1,)), ((), ()))
    travelling = negative_rows
    collected = jnp.zeros((negative_count, feature_count), jnp.float32)
    for turn_index in range(cycle_count):
        scores = lax.dot_general(
            queries, travelling, contract_cols, preferred_element_type=jnp.float32
        )
        weights = (scale_neg * jax.nn.sigmoid(scores)).astype(jnp.bfloat16)
        partner = partner + jnp.dot(weights, travelling, preferred_element_type=jnp.float32)
        collected = collected + lax.dot_general(
            weights, queries, contract_rows, preferred_element_type=jnp.float32
        )
        if turn_index + 1 < cycle_count:
            travelling = passed_along(travelling, "blk", 1)
        collected = passed_along(collected, "blk", 1)
    partner_low = partner.astype(jnp.bfloat16)
    spread_partner = partner_low[:, None, :] * relation_hot[:, :, None]
    head_grad = jnp.einsum(
        "ire,rde->id", spread_partner, relations, preferred_element_type=jnp.float32
    )
    tail_grad = slopes[:, None] * queries.astype(jnp.float32)
    rel_term = lax.dot_general(
        spread_heads, partner_low, contract_rows, preferred_element_type=jnp.float32
    )
    rel_term = rel_term.reshape(relation_count, feature_count, feature_count)
    row_grads = jnp.concatenate([head_grad, tail_grad, collected], axis=0)
    outgoing = (
        jnp.zeros((owner_count * capacity, feature_count), jnp.float32).at[target].set(row_grads)
    )
    outgoing = outgoing.reshape(owner_count, capacity, feature_count)
    returned = lax.all_to_all(outgoing, "owner", split_axis=0, concat_axis=0, tiled=True)
    shard_grad = jnp.zeros((entity_rows, feature_count), jnp.float32)
    shard_grad = shard_grad.at[asked_rows.reshape(-1)].add(returned.reshape(-1, feature_count))
    ent_grad = lax.psum_scatter(shard_grad, "blk", scatter_dimension=0, tiled=True)
    summed_all = lax.psum(rel_term, "owner")
    rel_grad = lax.psum_scatter(summed_all, "blk", scatter_dimension=0, tiled=True)
    return (ent_grad, rel_grad)


def solution(mesh):
    placed = (
        P("owner", None),
        P(),
        P(("owner", "blk")),
        P(("owner", "blk")),
        P(("owner", "blk")),
        P(("owner", "blk")),
    )
    return jax.shard_map(
        shards,
        mesh=mesh,
        in_specs=placed,
        out_specs=(P(("owner", "blk"), None), P("blk", None, None)),
        check_vma=False,
    )
```

profile of v0, /device:TPU:0, one launch (start us, length us, event | category | flops | bytes accessed | tf_op | source)
XLA Modules:
  0.0 458.3 jit_solution(10429002234024236272)
XLA Ops:
  7.2 0.8 constant_dynamic-update-slice_fusion.2
  8.0 0.7 fusion.47
  8.8 0.7 constant_dynamic-update-slice_fusion.1
  9.5 0.7 constant_dynamic-update-slice_fusion
  10.2 2.3 reduce-window.6
  12.5 0.3 slice_reduce_fusion
  13.1 0.8 fusion.45
  13.9 9.9 %scatter_custom_fusion = s32[6400]{0:T(1024)S(1)} fusion(s32[2560]{0:T(1024)S(1)} %fusion.45, s32[2560]{0:T(1024)S(1)} %get-tuple-element.2, s32[]{:T(128)} %constant.50.clone.1), kind=kCustom, calls=%fused_computation.77 | custom fusion | bytes 25604 | tf_op jit(solution)/shard_map/scatter | solution.py:31
  24.0 13.7 %all_to_all.25 = s32[8,1,800]{2,1,0:T(1,128)S(1)} all-to-all(s32[8,1,800]{2,1,0:T(1,128)S(1)} %all_to_all.16), channel_id=1, replica_groups=mesh['owner'=8,'blk'=4] {'owner'}, dimensions={0} | all-to-all | bytes 51200 | tf_op jit(solution)/shard_map/all_to_all | solution.py:33
  38.0 18.6 %gather_fusion = bf16[6400,256]{1,0:T(8,128)(2,1)} fusion(bf16[4096,256]{1,0:T(8,128)(2,1)S(1)} %copy-done, s32[7168]{0:T(1024)S(1)} %pad_clamp_fusion), kind=kCustom, calls=%fused_computation | custom fusion | bytes 6579200 | tf_op jit(solution)/shard_map/jit(_take)/gather | solution.py:34
  56.5 5.2 %broadcast_select_fusion = bf16[8,800,256]{2,1,0:T(8,128)(2,1)} fusion(bf16[8,800,256]{2,1,0:T(8,128)(2,1)} %bitcast.91, pred[8,800]{1,0:T(8,128)(4,1)S(1)} %compare_and_fusion), kind=kLoop, calls=%fused_computation.13 | loop fusion | flops 1638400 | bytes 6560000 | tf_op jit(solution)/shard_map/jit(_take)/select_n | solution.py:34
  61.7 4.6 %all-to-all-start.1 = ((bf16[8,800,256]{2,1,0:T(8,128)(2,1)}), bf16[8,800,256]{2,1,0:T(8,128)(2,1)}, u32[]{:S(2)}, u32[]{:S(2)}) async-start(bf16[8,800,256]{2,1,0:T(8,128)(2,1)} %broadcast_select_fusion), calls=%async_computation.1 | async-start | bytes 6553600 | tf_op jit(solution)/shard_map/all_to_all | solution.py:36
  66.4 72.3 %all-to-all-done.1 = bf16[8,800,256]{2,1,0:T(8,128)(2,1)} async-done(((bf16[8,800,256]{2,1,0:T(8,128)(2,1)}), bf16[8,800,256]{2,1,0:T(8,128)(2,1)}, u32[]{:S(2)}, u32[]{:S(2)}) %all-to-all-start.1) | async-done | bytes 3276832 | tf_op jit(solution)/shard_map/all_to_all | solution.py:36
  138.7 8.1 %gather_fusion.1 = bf16[2560,256]{1,0:T(8,128)(2,1)S(1)} fusion(bf16[6400,256]{1,0:T(8,128)(2,1)} %bitcast.6, s32[3072]{0:T(1024)S(1)} %pad_clamp_fusion.1), kind=kCustom, calls=%fused_computation.1 | custom fusion | bytes 2631680 | tf_op jit(solution)/shard_map/gather | solution.py:39
  146.8 0.7 slice.27
  147.5 0.8 slice.25
  148.3 2.1 copy.12
  150.4 2.8 fusion.30
  153.2 0.8 multiply_convert_fusion.3
  154.0 0.5 fusion.50
  154.5 0.4 convolution_add_fusion.3
  154.9 1.7 collective-permute-start.3
  156.8 1.7 multiply_convert_fusion.2
  158.6 1.4 convolution_add_fusion.2
  159.9 3.6 collective-permute-done.3
  163.6 0.5 convolution_add_fusion.4
  164.1 2.3 collective-permute-done.1
  166.4 0.8 multiply_convert_fusion.1
  167.1 0.4 convolution_add_fusion.1
  167.6 0.5 fusion.51
  168.1 4.6 %collective-permute-done.4 = f32[512,256]{1,0:T(8,128)S(1)} collective-permute-done((f32[512,256]{1,0:T(8,128)S(1)}, f32[512,256]{1,0:T(8,128)S(1)}, u32[]{:S(2)}, u32[]{:S(2)}) %collective-permute-start.4) | collective-permute-done | bytes 524320 | tf_op jit(solution)/shard_map/ppermute | solution.py:10
  173.0 2.5 collective-permute-done.2
  175.5 0.8 multiply_convert_fusion
  176.3 0.5 fusion.52
  176.8 4.9 %collective-permute-done.5 = f32[512,256]{1,0:T(8,128)S(1)} collective-permute-done((f32[512,256]{1,0:T(8,128)S(1)}, f32[512,256]{1,0:T(8,128)S(1)}, u32[]{:S(2)}, u32[]{:S(2)}) %collective-permute-start.5) | collective-permute-done | bytes 524320 | tf_op jit(solution)/shard_map/ppermute | solution.py:10
  181.6 0.9 add.138
  182.5 1.2 fusion.26
  183.7 2.1 copy.14
  185.8 3.7 fusion.20
  189.4 2.0 collective-permute-done.6
  191.4 15.5 %scatter_custom_fusion.1 = f32[6400,256]{1,0:T(8,128)} fusion(s32[2560]{0:T(1024)S(1)} %fusion.45, f32[]{:T(128)} %constant.49.clone.1, f32[512,256]{1,0:T(8,128)} %collective-permute-done.6, f32[]{:T(128)} %constant.68, f32[1024,256]{1,0:T(8,128)S(1)} %convert_multiply_fusion, f32[1024,256]{1,0:T(8,128)} %fusion.20), kind=kCustom, calls=%fused_computation.11 | custom fusion | flops 1310720 | bytes 9175048 | tf_op jit(solution)/shard_map/scatter | solution.py:85
  206.9 4.9 %all-to-all-start.2 = ((f32[8,800,256]{2,1,0:T(8,128)}), f32[8,800,256]{2,1,0:T(8,128)}, u32[]{:S(2)}, u32[]{:S(2)}) async-start(f32[8,800,256]{2,1,0:T(8,128)} %bitcast.90), calls=%async_computation.2 | async-start | bytes 13107200 | tf_op jit(solution)/shard_map/all_to_all | solution.py:88
  211.8 2.6 fusion.2
  214.5 33.4 %reduce-scatter.5.cloned.1.call-done = f32[2,256,256]{2,1,0:T(8,128)} async-done(((f32[8,256,256]{2,1,0:T(8,128)}), f32[2,256,256]{2,1,0:T(8,128)}) %reduce-scatter.5.cloned.1.call-update) | async-done | bytes 524304 | tf_op jit(solution)/shard_map/reduce_scatter | solution.py:93
  248.2 114.8 %all-to-all-done.2 = f32[8,800,256]{2,1,0:T(8,128)} async-done(((f32[8,800,256]{2,1,0:T(8,128)}), f32[8,800,256]{2,1,0:T(8,128)}, u32[]{:S(2)}, u32[]{:S(2)}) %all-to-all-start.2) | async-done | bytes 6553632 | tf_op jit(solution)/shard_map/all_to_all | solution.py:88
  363.0 44.3 %scatter_custom_fusion.2 = f32[4096,256]{1,0:T(8,128)} fusion(s32[6400]{0:T(1024)S(1)} %fusion.38, f32[6400,256]{1,0:T(8,128)} %bitcast.10, f32[]{:T(128)} %constant.49.clone.1), kind=kCustom, calls=%fused_computation.29 | custom fusion | flops 1638400 | bytes 4194816 | tf_op jit(solution)/shard_map/scatter-add | solution.py:90
  407.4 42.5 %reduce-scatter.3.cloned.1.call-done = f32[1024,256]{1,0:T(8,128)} async-done(((f32[4096,256]{1,0:T(8,128)}), f32[1024,256]{1,0:T(8,128)}) %reduce-scatter.3.cloned.1.call-update) | async-done | bytes 1048592 | tf_op jit(solution)/shard_map/reduce_scatter | solution.py:91
  449.9 1.9 copy.32
  (41 shorter events, 1.8 us)
Async XLA Ops:
  7.2 30.8 %copy-start = (bf16[4096,256]{1,0:T(8,128)(2,1)S(1)}, bf16[4096,256]{1,0:T(8,128)(2,1)}, u32[]{:S(2)}) copy-start(bf16[4096,256]{1,0:T(8,128)(2,1)} %param.6) | copy-start | bytes 6291460
  61.7 4.6 %copy-start.3 = (s32[1024]{0:T(1024)S(1)}, s32[1024]{0:T(1024)}, u32[]{:S(2)}) copy-start(s32[1024]{0:T(1024)} %param.9) | copy-start | bytes 12292
  61.7 77.0 %all-to-all-start.1 = ((bf16[8,800,256]{2,1,0:T(8,128)(2,1)}), bf16[8,800,256]{2,1,0:T(8,128)(2,1)}, u32[]{:S(2)}, u32[]{:S(2)}) async-start(bf16[8,800,256]{2,1,0:T(8,128)(2,1)} %broadcast_select_fusion), calls=%async_computation.1 | async-start | bytes 6553600 | tf_op jit(solution)/shard_map/all_to_all | solution.py:36
  148.3 8.4 %collective-permute-start = (bf16[512,256]{1,0:T(8,128)(2,1)}, bf16[512,256]{1,0:T(8,128)(2,1)}, u32[]{:S(2)}, u32[]{:S(2)}) collective-permute-start(bf16[512,256]{1,0:T(8,128)(2,1)} %slice.27), channel_id=1, source_target_pairs={{3,0},{0,1},{1,2},{2,3},{7,4},{4,5},{5,6},{6,7},{11,8},{8,9},{9,10... | collective-permute-start | bytes 786440 | tf_op jit(solution)/shard_map/ppermute | solution.py:10
  154.9 8.7 %collective-permute-start.3 = (f32[512,256]{1,0:T(8,128)S(1)}, f32[512,256]{1,0:T(8,128)S(1)}, u32[]{:S(2)}, u32[]{:S(2)}) collective-permute-start(f32[512,256]{1,0:T(8,128)S(1)} %fusion.50), channel_id=1, source_target_pairs={{3,0},{0,1},{1,2},{2,3},{7,4},{4,5},{5,6},{6,7},{11,8},{8,9},{9,10... | collective-permute-start | bytes 1572872 | tf_op jit(solution)/shard_map/ppermute | solution.py:10
  156.8 9.6 %collective-permute-start.1 = (bf16[512,256]{1,0:T(8,128)(2,1)}, bf16[512,256]{1,0:T(8,128)(2,1)S(1)}, u32[]{:S(2)}, u32[]{:S(2)}) collective-permute-start(bf16[512,256]{1,0:T(8,128)(2,1)} %collective-permute-done), channel_id=1, source_target_pairs={{3,0},{0,1},{1,2},{2,3},{7,4},{4,5},{5,6},{6,7},{11,8},{8,9},{9,10... | collective-permute-start | bytes 786440 | tf_op jit(solution)/shard_map/ppermute | solution.py:10
  164.1 8.7 %collective-permute-start.4 = (f32[512,256]{1,0:T(8,128)S(1)}, f32[512,256]{1,0:T(8,128)S(1)}, u32[]{:S(2)}, u32[]{:S(2)}) collective-permute-start(f32[512,256]{1,0:T(8,128)S(1)} %convolution_add_fusion.4), channel_id=1, source_target_pairs={{3,0},{0,1},{1,2},{2,3},{7,4},{4,5},{5,6},{6,7},{11,8},{8,9},{9,10... | collective-permute-start | bytes 1572872 | tf_op jit(solution)/shard_map/ppermute | solution.py:10
  166.4 9.1 %collective-permute-start.2 = (bf16[512,256]{1,0:T(8,128)(2,1)S(1)}, bf16[512,256]{1,0:T(8,128)(2,1)S(1)}, u32[]{:S(2)}, u32[]{:S(2)}) collective-permute-start(bf16[512,256]{1,0:T(8,128)(2,1)S(1)} %collective-permute-done.1), channel_id=1, source_target_pairs={{3,0},{0,1},{1,2},{2,3},{7,4},{4,5},{5,6},{6,7},{11,8},{8,9},{9,10... | collective-permute-start | bytes 786440 | tf_op jit(solution)/shard_map/ppermute | solution.py:10
  172.8 8.8 %collective-permute-start.5 = (f32[512,256]{1,0:T(8,128)S(1)}, f32[512,256]{1,0:T(8,128)S(1)}, u32[]{:S(2)}, u32[]{:S(2)}) collective-permute-start(f32[512,256]{1,0:T(8,128)S(1)} %add.137), channel_id=1, source_target_pairs={{3,0},{0,1},{1,2},{2,3},{7,4},{4,5},{5,6},{6,7},{11,8},{8,9},{9,10... | collective-permute-start | bytes 1572872 | tf_op jit(solution)/shard_map/ppermute | solution.py:10
  182.5 8.9 %collective-permute-start.6 = (f32[512,256]{1,0:T(8,128)}, f32[512,256]{1,0:T(8,128)}, u32[]{:S(2)}, u32[]{:S(2)}) collective-permute-start(f32[512,256]{1,0:T(8,128)} %add.138), channel_id=1, source_target_pairs={{3,0},{0,1},{1,2},{2,3},{7,4},{4,5},{5,6},{6,7},{11,8},{8,9},{9,10... | collective-permute-start | bytes 1572872 | tf_op jit(solution)/shard_map/ppermute | solution.py:10
  206.9 5.0 %copy-start.1 = (bf16[1024,256]{1,0:T(8,128)(2,1)S(1)}, bf16[1024,256]{1,0:T(8,128)(2,1)}, u32[]{:S(2)}) copy-start(bf16[1024,256]{1,0:T(8,128)(2,1)} %fusion.26) | copy-start | bytes 1572868
  206.9 5.0 %copy-start.2 = (bf16[1024,256]{0,1:T(8,128)(2,1)S(1)}, bf16[1024,256]{0,1:T(8,128)(2,1)}, u32[]{:S(2)}) copy-start(bf16[1024,256]{0,1:T(8,128)(2,1)} %copy.12) | copy-start | bytes 1572868
  206.9 156.1 %all-to-all-start.2 = ((f32[8,800,256]{2,1,0:T(8,128)}), f32[8,800,256]{2,1,0:T(8,128)}, u32[]{:S(2)}, u32[]{:S(2)}) async-start(f32[8,800,256]{2,1,0:T(8,128)} %bitcast.90), calls=%async_computation.2 | async-start | bytes 13107200 | tf_op jit(solution)/shard_map/all_to_all | solution.py:88
  211.8 36.1 %reduce-scatter.5.cloned.1.call-start = ((), (), s32[]{:S(2)}) async-start(), calls=%async_computation.6 | async-start | bytes 2621440 | tf_op jit(solution)/shard_map/reduce_scatter | solution.py:93
  214.4 192.9 %all-reduce.2.cloned.1.call-start = ((), (), s32[]{:S(2)}) async-start(), calls=%async_computation.7 | async-start | bytes 1048576 | tf_op jit(solution)/shard_map/psum | solution.py:92
  247.9 202.0 %reduce-scatter.3.cloned.1.call-start = ((), (), s32[]{:S(2)}) async-start(), calls=%async_computation.5 | async-start | bytes 5242880 | tf_op jit(solution)/shard_map/reduce_scatter | solution.py:91
Sparse Core Ops, SparseCore 0:
  215.1 32.7 reduce-scatter.4
  251.7 151.0 all-reduce.1
  407.5 42.3 reduce-scatter.2
where the time goes:
time: 459 us; the launch traced here: 458 us
  waiting for transfers between devices  283 us (62%)
  other arithmetic  70.6 us (15%)
  local copies, waits for them, and re-layouts  47 us (10%)
  matrix products  18.3 us (4%)
  between operations  14.1 us (3%)
  blocking collectives  13.7 us (3%)
  starting transfers between devices  11.6 us (3%)
    all_to_all x1, waiting for transfers between devices, shards(): lax.all_to_all(outgoing, 'owner', split_axis=0, concat_axis=0, tiled=True)  115 us
    all_to_all x1, waiting for transfers between devices, shards(): lax.all_to_all(found_rows, 'owner', split_axis=0, concat_axis=0, tiled=True)  72.3 us
    scatter-add x1, other arithmetic, shards(): shard_grad.at[asked_rows.reshape(-1)]  44.3 us
    reduce_scatter x1, waiting for transfers between devices, shards(): lax.psum_scatter(shard_grad, 'blk', scatter_dimension=0, tiled=True)  42.5 us
    reduce_scatter x1, waiting for transfers between devices, shards(): lax.psum_scatter(summed_all, 'blk', scatter_dimension=0, tiled=True)  33.4 us
    ppermute x7, waiting for transfers between devices, passed_along(): return lax.ppermute(block, axis, route)  19.9 us
    gather x1, local copies, waits for them, and re-layouts, shards(): found_rows = jnp.take(entity_table, asked_rows, axis=0)  18.6 us
    scatter x1, other arithmetic, shards(): jnp.zeros((owner_count * capacity, feature_count), jnp.float32).at[target]  15.5 us
  transfers between devices with their start and end apart: 12, of which 10 were waited for; matrix products, arithmetic and copies ran while one was open for 15% of the time, Pallas kernels for 0%

commit v1 on v0

--- a/solution.py
+++ b/solution.py
@@ -8,6 +8,22 @@
     devices = range(lax.axis_size(axis))
     route = [((i - distance) % len(devices), i) for i in devices]
     return lax.ppermute(block, axis, route)
+
+
+def earlier(count):
+    place = jnp.arange(count, dtype=jnp.int32)
+    return (place[:, None] > place[None, :]).astype(jnp.bfloat16)
+
+
+def ranks(onehot):
+    ids, owner_count = onehot.shape
+    run = 128
+    runs = onehot.reshape(ids // run, run, owner_count)
+    within = jnp.einsum("ij,bjo->bio", earlier(run), runs, preferred_element_type=jnp.float32)
+    totals = jnp.sum(runs.astype(jnp.float32), axis=1).astype(jnp.bfloat16)
+    carried = jnp.dot(earlier(ids // run), totals, preferred_element_type=jnp.float32)
+    before = within + carried[:, None, :]
+    return jnp.sum(before * runs.astype(jnp.float32), axis=2).reshape(ids).astype(jnp.int32)
 
 
 def shards(entity_table, relations, head_ids, rel_ids, tail_ids, neg_ids):
@@ -23,13 +39,15 @@
     owners = wanted // entity_rows
     local_rows = wanted % entity_rows
     onehot = (owners[:, None] == jnp.arange(owner_count, dtype=jnp.int32)[None, :]).astype(
-        jnp.int32
+        jnp.bfloat16
     )
-    before = jnp.cumsum(onehot, axis=0) - onehot
-    slot_index = jnp.sum(before * onehot, axis=1)
+    slot_index = ranks(onehot)
     target = owners * capacity + slot_index
-    requests = jnp.zeros((owner_count * capacity,), jnp.int32).at[target].set(local_rows)
-    requests = requests.reshape(owner_count, capacity)
+    slots = jnp.arange(owner_count * capacity, dtype=jnp.int32)
+    packing = (slots[:, None] == target[None, :]).astype(jnp.bfloat16)
+    digits = jnp.stack([local_rows // 64, local_rows % 64], axis=1).astype(jnp.bfloat16)
+    packed = jnp.dot(packing, digits, preferred_element_type=jnp.float32).astype(jnp.int32)
+    requests = (packed[:, 0] * 64 + packed[:, 1]).reshape(owner_count, capacity)
     asked_rows = lax.all_to_all(requests, "owner", split_axis=0, concat_axis=0, tiled=True)
     found_rows = jnp.take(entity_table, asked_rows, axis=0)
     fetched, asked_rows = (
@@ -81,16 +99,20 @@
     )
     rel_term = rel_term.reshape(relation_count, feature_count, feature_count)
     row_grads = jnp.concatenate([head_grad, tail_grad, collected], axis=0)
-    outgoing = (
-        jnp.zeros((owner_count * capacity, feature_count), jnp.float32).at[target].set(row_grads)
-    )
+    outgoing = jnp.dot(
+        packing, row_grads.astype(jnp.bfloat16), preferred_element_type=jnp.float32
+    ).astype(jnp.bfloat16)
     outgoing = outgoing.reshape(owner_count, capacity, feature_count)
     returned = lax.all_to_all(outgoing, "owner", split_axis=0, concat_axis=0, tiled=True)
-    shard_grad = jnp.zeros((entity_rows, feature_count), jnp.float32)
-    shard_grad = shard_grad.at[asked_rows.reshape(-1)].add(returned.reshape(-1, feature_count))
+    landing = (
+        jnp.arange(entity_rows, dtype=jnp.int32)[:, None] == asked_rows.reshape(-1)[None, :]
+    ).astype(jnp.bfloat16)
+    shard_grad = jnp.dot(
+        landing, returned.reshape(-1, feature_count), preferred_element_type=jnp.float32
+    )
     ent_grad = lax.psum_scatter(shard_grad, "blk", scatter_dimension=0, tiled=True)
-    summed_all = lax.psum(rel_term, "owner")
-    rel_grad = lax.psum_scatter(summed_all, "blk", scatter_dimension=0, tiled=True)
+    summed_group = lax.psum_scatter(rel_term, "blk", scatter_dimension=0, tiled=True)
+    rel_grad = lax.psum(summed_group, "owner")
     return (ent_grad, rel_grad)
 
 

time: 459 us -> 401 us (0.87)
  other arithmetic: 70.6 us -> 9.66 us
  matrix products: 18.3 us -> 61.7 us
  waiting for transfers between devices: 283 us -> 253 us
  local copies, waits for them, and re-layouts: 47 us -> 36.1 us
    all_to_all x1, waiting for transfers between devices: 115 us -> 42.5 us  [shards(): lax.all_to_all(outgoing, 'owner', split_axis=0, concat_axis=0, tiled=True)]
    dot_general x0 -> x5, matrix products: none -> 47 us  [the longest x1 21.4 us: shards(): jnp.dot(landing, returned.reshape(-1, feature_count), preferred_element_t...]
    scatter-add x1 -> x0, other arithmetic: 44.3 us -> none  [shards(): shard_grad.at[asked_rows.reshape(-1)]]
    psum x1, waiting for transfers between devices: 0.02 us -> 32.2 us  [shards(): rel_grad = lax.psum(summed_group, 'owner')]
    scatter x1 -> x0, other arithmetic: 15.5 us -> none  [shards(): jnp.zeros((owner_count * capacity, feature_count), jnp.float32).at[target]]
    scatter x1 -> x0, local copies, waits for them, and re-layouts: 9.95 us -> none  [shards(): jnp.zeros((owner_count * capacity,), jnp.int32).at[target].set(local_rows)]
    ppermute x7, waiting for transfers between devices: 19.9 us -> 26.2 us  [passed_along(): return lax.ppermute(block, axis, route)]
  transfers between devices with their start and end apart: 12 -> 12, of which waited for: 10 -> 11; matrix products, arithmetic and copies ran while one was open for 15% -> 9% of each run, Pallas kernels for 0% -> 0%
where the time goes in v1:
time: 401 us; the launch traced here: 400 us
  waiting for transfers between devices  253 us (63%)
  matrix products  61.7 us (15%)
  local copies, waits for them, and re-layouts  36.1 us (9%)
  between operations  14.1 us (4%)
  blocking collectives  13.7 us (3%)
  starting transfers between devices  11.4 us (3%)
  other arithmetic  9.66 us (2%)
    all_to_all x1, waiting for transfers between devices, shards(): lax.all_to_all(found_rows, 'owner', split_axis=0, concat_axis=0, tiled=True)  72.3 us
    reduce_scatter x1, waiting for transfers between devices, shards(): lax.psum_scatter(shard_grad, 'blk', scatter_dimension=0, tiled=True)  46.9 us
    all_to_all x1, waiting for transfers between devices, shards(): lax.all_to_all(outgoing, 'owner', split_axis=0, concat_axis=0, tiled=True)  42.5 us
    reduce_scatter x1, waiting for transfers between devices, shards(): lax.psum_scatter(rel_term, 'blk', scatter_dimension=0, tiled=True)  33.2 us
    psum x1, waiting for transfers between devices, shards(): rel_grad = lax.psum(summed_group, 'owner')  32.2 us
    ppermute x7, waiting for transfers between devices, passed_along(): return lax.ppermute(block, axis, route)  26.2 us
    dot_general x1, matrix products, shards(): jnp.dot(landing, returned.reshape(-1, feature_count), preferred_element_t...  21.4 us
    gather x1, local copies, waits for them, and re-layouts, shards(): found_rows = jnp.take(entity_table, asked_rows, axis=0)  18.6 us
  transfers between devices with their start and end apart: 12, of which 11 were waited for; matrix products, arithmetic and copies ran while one was open for 9% of the time, Pallas kernels for 0%

profile of v1, /device:TPU:0, one launch (start us, length us, event | category | flops | bytes accessed | tf_op | source)
XLA Modules:
  0.0 400.1 jit_solution(17364616361421414204)
XLA Ops:
  7.2 0.8 constant_dynamic-update-slice_fusion.2
  8.0 0.8 fusion.69
  9.4 0.7 constant_dynamic-update-slice_fusion.1
  10.1 0.7 constant_dynamic-update-slice_fusion
  10.8 11.4 %fusion.7 = s32[6400,2]{0,1:T(2,128)S(1)} fusion(s32[2560]{0:T(1024)S(1)} %fusion.53, bf16[2560,1]{0,1:T(2,128)(2,1)S(1)} %fusion.60, bf16[2560,1]{0,1:T(2,128)(2,1)S(1)} %get-tuple-element.4), kind=kOutput, calls=%fused_computation.11 | convolution fusion | flops 81953280 | bytes 71680 | tf_op jit(solution)/shard_map/dot_general | solution.py:49
  22.5 13.7 %all_to_all.22 = s32[8,1,800]{2,1,0:T(1,128)S(1)} all-to-all(s32[8,1,800]{2,1,0:T(1,128)S(1)} %add.196), channel_id=1, replica_groups=mesh['owner'=8,'blk'=4] {'owner'}, dimensions={0} | all-to-all | bytes 51200 | tf_op jit(solution)/shard_map/all_to_all | solution.py:51
  36.4 18.6 %gather_fusion = bf16[6400,256]{1,0:T(8,128)(2,1)} fusion(bf16[4096,256]{1,0:T(8,128)(2,1)S(1)} %copy-done, s32[7168]{0:T(1024)S(1)} %pad_clamp_fusion), kind=kCustom, calls=%fused_computation | custom fusion | bytes 6579200 | tf_op jit(solution)/shard_map/jit(_take)/gather | solution.py:52
  55.0 5.2 %broadcast_select_fusion = bf16[8,800,256]{2,1,0:T(8,128)(2,1)} fusion(bf16[8,800,256]{2,1,0:T(8,128)(2,1)} %bitcast.92, pred[8,800]{1,0:T(8,128)(4,1)S(1)} %compare_and_fusion), kind=kLoop, calls=%fused_computation.18 | loop fusion | flops 1638400 | bytes 6560000 | tf_op jit(solution)/shard_map/jit(_take)/select_n | solution.py:52
  60.2 4.6 %all-to-all-start.1 = ((bf16[8,800,256]{2,1,0:T(8,128)(2,1)}), bf16[8,800,256]{2,1,0:T(8,128)(2,1)}, u32[]{:S(2)}, u32[]{:S(2)}) async-start(bf16[8,800,256]{2,1,0:T(8,128)(2,1)} %broadcast_select_fusion), calls=%async_computation.1 | async-start | bytes 6553600 | tf_op jit(solution)/shard_map/all_to_all | solution.py:54
  64.9 72.3 %all-to-all-done.1 = bf16[8,800,256]{2,1,0:T(8,128)(2,1)} async-done(((bf16[8,800,256]{2,1,0:T(8,128)(2,1)}), bf16[8,800,256]{2,1,0:T(8,128)(2,1)}, u32[]{:S(2)}, u32[]{:S(2)}) %all-to-all-start.1) | async-done | bytes 3276832 | tf_op jit(solution)/shard_map/all_to_all | solution.py:54
  137.2 8.1 %gather_fusion.1 = bf16[2560,256]{1,0:T(8,128)(2,1)S(1)} fusion(bf16[6400,256]{1,0:T(8,128)(2,1)} %bitcast.8, s32[3072]{0:T(1024)S(1)} %pad_clamp_fusion.1), kind=kCustom, calls=%fused_computation.1 | custom fusion | bytes 2631680 | tf_op jit(solution)/shard_map/gather | solution.py:57
  145.3 0.8 slice.26
  146.1 0.7 slice.28
  146.8 2.0 copy.15
  148.9 2.8 fusion.40
  151.7 0.7 multiply_convert_fusion.3
  152.8 0.4 convolution_add_fusion.3
  153.2 0.5 fusion.70
  153.7 1.7 collective-permute-start.3
  155.4 1.0 fusion.41
  156.3 2.2 collective-permute-done
  158.6 0.8 multiply_convert_fusion.2
  159.3 0.4 convolution_add_fusion.2
  159.8 4.4 %collective-permute-done.3 = f32[512,256]{1,0:T(8,128)S(1)} collective-permute-done((f32[512,256]{1,0:T(8,128)S(1)}, f32[512,256]{1,0:T(8,128)S(1)}, u32[]{:S(2)}, u32[]{:S(2)}) %collective-permute-start.3) | collective-permute-done | bytes 524320 | tf_op jit(solution)/shard_map/ppermute | solution.py:10
  164.2 0.5 convolution_add_fusion.4
  164.7 2.3 collective-permute-done.1
  167.0 0.8 multiply_convert_fusion.1
  167.8 0.4 convolution_add_fusion.1
  168.3 0.5 fusion.71
  168.7 7.4 %collective-permute-done.2 = bf16[512,256]{1,0:T(8,128)(2,1)S(1)} collective-permute-done((bf16[512,256]{1,0:T(8,128)(2,1)S(1)}, bf16[512,256]{1,0:T(8,128)(2,1)S(1)}, u32[]{:S(2)}, u32[]{:S(2)}) %collective-permute-start.2) | collective-permute-done | bytes 262176 | tf_op jit(solution)/shard_map/ppermute | solution.py:10
  176.1 0.7 multiply_convert_fusion
  176.9 1.0 add.193
  178.0 0.4 fusion.30
  178.5 1.0 copy.17
  179.5 1.8 fusion.72
  181.3 5.5 %collective-permute-done.5 = f32[512,256]{1,0:T(8,128)} collective-permute-done((f32[512,256]{1,0:T(8,128)}, f32[512,256]{1,0:T(8,128)}, u32[]{:S(2)}, u32[]{:S(2)}) %collective-permute-start.5) | collective-permute-done | bytes 524320 | tf_op jit(solution)/shard_map/ppermute | solution.py:10
  186.8 1.1 add.194
  188.0 1.4 fusion.34
  189.4 4.4 %collective-permute-done.6 = bf16[512,256]{1,0:T(8,128)(2,1)S(1)} collective-permute-done((bf16[512,256]{1,0:T(8,128)(2,1)S(1)}, bf16[512,256]{1,0:T(8,128)(2,1)S(1)}, u32[]{:S(2)}, u32[]{:S(2)}) %collective-permute-start.6) | collective-permute-done | bytes 262176 | tf_op jit(solution)/shard_map/ppermute | solution.py:10
  193.8 13.8 %fusion.6 = bf16[6400,256]{1,0:T(8,128)(2,1)} fusion(s32[2560]{0:T(1024)S(1)} %fusion.53, bf16[512,256]{1,0:T(8,128)(2,1)S(1)} %collective-permute-done.6, bf16[1024,256]{1,0:T(8,128)(2,1)S(1)} %copy-done.5, bf16[1024,256]{1,0:T(8,128)(2,1)S(1)} %fusion.34), kind=kOutput, calls=%fused_computation.10 | convolution fusion | flops 8410562560 | bytes 4597760 | tf_op jit(solution)/shard_map/dot_general | solution.py:102
  207.6 4.6 %all-to-all-start.2 = ((bf16[8,800,256]{2,1,0:T(8,128)(2,1)}), bf16[8,800,256]{2,1,0:T(8,128)(2,1)}, u32[]{:S(2)}, u32[]{:S(2)}) async-start(bf16[8,800,256]{2,1,0:T(8,128)(2,1)} %bitcast.93), calls=%async_computation.2 | async-start | bytes 6553600 | tf_op jit(solution)/shard_map/all_to_all | solution.py:106
  212.2 2.7 fusion.10
  215.1 33.2 %reduce-scatter.5.cloned.1.call-done = f32[2,256,256]{2,1,0:T(8,128)} async-done(((f32[8,256,256]{2,1,0:T(8,128)}), f32[2,256,256]{2,1,0:T(8,128)}) %reduce-scatter.5.cloned.1.call-update) | async-done | bytes 524304 | tf_op jit(solution)/shard_map/reduce_scatter | solution.py:114
  248.6 42.5 %all-to-all-done.2 = bf16[8,800,256]{2,1,0:T(8,128)(2,1)} async-done(((bf16[8,800,256]{2,1,0:T(8,128)(2,1)}), bf16[8,800,256]{2,1,0:T(8,128)(2,1)}, u32[]{:S(2)}, u32[]{:S(2)}) %all-to-all-start.2) | async-done | bytes 3276832 | tf_op jit(solution)/shard_map/all_to_all | solution.py:106
  291.1 21.4 %fusion = f32[4096,256]{1,0:T(8,128)} fusion(bf16[6400,256]{1,0:T(8,128)(2,1)} %bitcast.12, s32[6400]{0:T(1024)S(1)} %eq.70), kind=kOutput, calls=%fused_computation.3 | convolution fusion | flops 13447987200 | bytes 7496704 | tf_op jit(solution)/shard_map/dot_general | solution.py:110
  312.6 32.2 %all-reduce.2.cloned.1.call-done = f32[2,256,256]{2,1,0:T(8,128)} async-done(((f32[2,256,256]{2,1,0:T(8,128)}), f32[2,256,256]{2,1,0:T(8,128)}) %all-reduce.2.cloned.1.call-update) | async-done | bytes 524304 | tf_op jit(solution)/shard_map/psum | solution.py:115
  344.8 46.9 %reduce-scatter.3.cloned.1.call-done = f32[1024,256]{1,0:T(8,128)} async-done(((f32[4096,256]{1,0:T(8,128)}), f32[1024,256]{1,0:T(8,128)}) %reduce-scatter.3.cloned.1.call-update) | async-done | bytes 1048592 | tf_op jit(solution)/shard_map/reduce_scatter | solution.py:113
  391.7 1.9 copy.36
  (53 shorter events, 2.2 us)
Async XLA Ops:
  7.2 29.2 %copy-start = (bf16[4096,256]{1,0:T(8,128)(2,1)S(1)}, bf16[4096,256]{1,0:T(8,128)(2,1)}, u32[]{:S(2)}) copy-start(bf16[4096,256]{1,0:T(8,128)(2,1)} %param.6) | copy-start | bytes 6291460
  60.2 4.6 %copy-start.8 = (s32[1024]{0:T(1024)S(1)}, s32[1024]{0:T(1024)}, u32[]{:S(2)}) copy-start(s32[1024]{0:T(1024)} %param.9) | copy-start | bytes 12292
  60.2 77.0 %all-to-all-start.1 = ((bf16[8,800,256]{2,1,0:T(8,128)(2,1)}), bf16[8,800,256]{2,1,0:T(8,128)(2,1)}, u32[]{:S(2)}, u32[]{:S(2)}) async-start(bf16[8,800,256]{2,1,0:T(8,128)(2,1)} %broadcast_select_fusion), calls=%async_computation.1 | async-start | bytes 6553600 | tf_op jit(solution)/shard_map/all_to_all | solution.py:54
  151.6 24.5 %copy-start.1 = (bf16[1024,256]{1,0:T(8,128)(2,1)}, bf16[1024,256]{1,0:T(8,128)(2,1)S(1)}, u32[]{:S(2)}) copy-start(bf16[1024,256]{1,0:T(8,128)(2,1)S(1)} %get-tuple-element.9) | copy-start | bytes 1572868
  151.7 1.1 copy-start.7
  152.8 5.8 %collective-permute-start = (bf16[512,256]{1,0:T(8,128)(2,1)S(1)}, bf16[512,256]{1,0:T(8,128)(2,1)S(1)}, u32[]{:S(2)}, u32[]{:S(2)}) collective-permute-start(bf16[512,256]{1,0:T(8,128)(2,1)S(1)} %copy-done.7), channel_id=1, source_target_pairs={{3,0},{0,1},{1,2},{2,3},{7,4},{4,5},{5,6},{6,7},{11,8},{8,9},{9,10... | collective-permute-start | bytes 786440 | tf_op jit(solution)/shard_map/ppermute | solution.py:10
  153.7 10.5 %collective-permute-start.3 = (f32[512,256]{1,0:T(8,128)S(1)}, f32[512,256]{1,0:T(8,128)S(1)}, u32[]{:S(2)}, u32[]{:S(2)}) collective-permute-start(f32[512,256]{1,0:T(8,128)S(1)} %fusion.70), channel_id=1, source_target_pairs={{3,0},{0,1},{1,2},{2,3},{7,4},{4,5},{5,6},{6,7},{11,8},{8,9},{9,10... | collective-permute-start | bytes 1572872 | tf_op jit(solution)/shard_map/ppermute | solution.py:10
  158.6 8.4 %collective-permute-start.1 = (bf16[512,256]{1,0:T(8,128)(2,1)S(1)}, bf16[512,256]{1,0:T(8,128)(2,1)S(1)}, u32[]{:S(2)}, u32[]{:S(2)}) collective-permute-start(bf16[512,256]{1,0:T(8,128)(2,1)S(1)} %collective-permute-done), channel_id=1, source_target_pairs={{3,0},{0,1},{1,2},{2,3},{7,4},{4,5},{5,6},{6,7},{11,8},{8,9},{9,10... | collective-permute-start | bytes 786440 | tf_op jit(solution)/shard_map/ppermute | solution.py:10
  164.7 12.2 %collective-permute-start.4 = (f32[512,256]{1,0:T(8,128)S(1)}, f32[512,256]{1,0:T(8,128)S(1)}, u32[]{:S(2)}, u32[]{:S(2)}) collective-permute-start(f32[512,256]{1,0:T(8,128)S(1)} %convolution_add_fusion.4), channel_id=1, source_target_pairs={{3,0},{0,1},{1,2},{2,3},{7,4},{4,5},{5,6},{6,7},{11,8},{8,9},{9,10... | collective-permute-start | bytes 1572872 | tf_op jit(solution)/shard_map/ppermute | solution.py:10
  167.8 8.4 %collective-permute-start.2 = (bf16[512,256]{1,0:T(8,128)(2,1)S(1)}, bf16[512,256]{1,0:T(8,128)(2,1)S(1)}, u32[]{:S(2)}, u32[]{:S(2)}) collective-permute-start(bf16[512,256]{1,0:T(8,128)(2,1)S(1)} %collective-permute-done.1), channel_id=1, source_target_pairs={{3,0},{0,1},{1,2},{2,3},{7,4},{4,5},{5,6},{6,7},{11,8},{8,9},{9,10... | collective-permute-start | bytes 786440 | tf_op jit(solution)/shard_map/ppermute | solution.py:10
  176.9 1.1 copy-start.3
  177.9 1.6 copy-start.2
  177.9 8.9 %collective-permute-start.5 = (f32[512,256]{1,0:T(8,128)}, f32[512,256]{1,0:T(8,128)}, u32[]{:S(2)}, u32[]{:S(2)}) collective-permute-start(f32[512,256]{1,0:T(8,128)} %add.193), channel_id=1, source_target_pairs={{3,0},{0,1},{1,2},{2,3},{7,4},{4,5},{5,6},{6,7},{11,8},{8,9},{9,10... | collective-permute-start | bytes 1572872 | tf_op jit(solution)/shard_map/ppermute | solution.py:10
  179.5 8.5 %copy-start.6 = (bf16[1024,256]{0,1:T(8,128)(2,1)S(1)}, bf16[1024,256]{0,1:T(8,128)(2,1)}, u32[]{:S(2)}) copy-start(bf16[1024,256]{0,1:T(8,128)(2,1)} %copy.17) | copy-start | bytes 1572868
  179.5 8.5 %copy-start.9 = (bf16[8,256,256]{2,1,0:T(8,128)(2,1)S(1)}, bf16[8,256,256]{2,1,0:T(8,128)(2,1)}, u32[]{:S(2)}) copy-start(bf16[8,256,256]{2,1,0:T(8,128)(2,1)} %param.7) | copy-start | bytes 3145732
  187.9 5.9 %copy-start.5 = (bf16[1024,256]{1,0:T(8,128)(2,1)S(1)}, bf16[1024,256]{1,0:T(8,128)(2,1)}, u32[]{:S(2)}) copy-start(bf16[1024,256]{1,0:T(8,128)(2,1)} %fusion.41) | copy-start | bytes 1572868
  188.0 5.8 %collective-permute-start.6 = (bf16[512,256]{1,0:T(8,128)(2,1)S(1)}, bf16[512,256]{1,0:T(8,128)(2,1)S(1)}, u32[]{:S(2)}, u32[]{:S(2)}) collective-permute-start(bf16[512,256]{1,0:T(8,128)(2,1)S(1)} %add.194), channel_id=1, source_target_pairs={{3,0},{0,1},{1,2},{2,3},{7,4},{4,5},{5,6},{6,7},{11,8},{8,9},{9,10... | collective-permute-start | bytes 786440 | tf_op jit(solution)/shard_map/ppermute | solution.py:10
  207.6 4.6 %copy-start.4 = (bf16[1024,256]{0,1:T(8,128)(2,1)S(1)}, bf16[1024,256]{0,1:T(8,128)(2,1)}, u32[]{:S(2)}) copy-start(bf16[1024,256]{0,1:T(8,128)(2,1)} %copy.15) | copy-start | bytes 1572868
  207.6 83.5 %all-to-all-start.2 = ((bf16[8,800,256]{2,1,0:T(8,128)(2,1)}), bf16[8,800,256]{2,1,0:T(8,128)(2,1)}, u32[]{:S(2)}, u32[]{:S(2)}) async-start(bf16[8,800,256]{2,1,0:T(8,128)(2,1)} %bitcast.93), calls=%async_computation.2 | async-start | bytes 6553600 | tf_op jit(solution)/shard_map/all_to_all | solution.py:106
  212.2 36.2 %reduce-scatter.5.cloned.1.call-start = ((), (), s32[]{:S(2)}) async-start(), calls=%async_computation.6 | async-start | bytes 2621440 | tf_op jit(solution)/shard_map/reduce_scatter | solution.py:114
  214.9 129.9 %all-reduce.2.cloned.1.call-start = ((), (), s32[]{:S(2)}) async-start(), calls=%async_computation.7 | async-start | bytes 1048576 | tf_op jit(solution)/shard_map/psum | solution.py:115
  248.4 143.4 %reduce-scatter.3.cloned.1.call-start = ((), (), s32[]{:S(2)}) async-start(), calls=%async_computation.5 | async-start | bytes 5242880 | tf_op jit(solution)/shard_map/reduce_scatter | solution.py:113
Sparse Core Ops, SparseCore 0:
  215.5 32.7 reduce-scatter.4
  252.1 92.6 all-reduce.1
  347.9 43.7 reduce-scatter.2
